TPU v7x, 32 devices: a whole 2x2x4 slice. The times are simulated.
32 devices in a mesh: region: 4 (over z), sub: 8 (over y, x, core).
Axes of the slice: x: 2, y: 2, z: 4, core: 2. Of those that a mesh axis runs over, the one named last changes fastest.
Arguments:
- members: bfloat16 [1024, 65536], P(('region', 'sub'))
- obs_perturb: bfloat16 [8192, 1024], P(('region', 'sub')), may hold values from -6 to 6
- innovations: bfloat16 [8192], P(('region', 'sub')), may hold values from -12 to 12
- obs_list: int32 [32, 2048], P(('region', 'sub')), may hold values from 0 to 2047, as said below
- obs_blocks: int32 [32], P(('region', 'sub')), may hold values from 8 to 16, as said below
- obs_precision: float32 [32, 2048], P(('region', 'sub')), may hold values from 0.1 to 1
- interp_slots: int32 [2048, 2], P(('region', 'sub')), may hold values from 0 to 2, as said below
- interp_weight: float32 [2048], P(('region', 'sub')), may hold values from 0.2 to 0.8
Outputs:
- analysis: bfloat16 [1024, 65536], P(None, ('region', 'sub'))
Inputs may be any that keep to these rules, and one draw needn't show every extreme that they name: `obs_list`: the 2048 entries of a point's list are distinct. Entries from obs_blocks * 128 on are padding; some point uses all 2048 entries. `interp_slots`: the two slots of a column differ.
All inputs are finite; a program needn't handle non-finite values.
Results may differ from a plain program's by a relative error of at most 0.0058.
Values may be sent and summed in bfloat16 or wider, within the bound.
A program may use at most 128 MiB of HBM per device.

v0:
```python
import jax
import jax.numpy as jnp
from jax import lax
from jax.experimental import pallas as pl
from jax.experimental.pallas import tpu as pltpu
from jax.sharding import PartitionSpec as P

LEV = 8
VARS = 4
BLOCK = 128
EXTRA = 16
TILE = 256
VMEM_BYTES = 60 * 1024 * 1024
POLY = (1.38671875, -1.140625, 0.9375, -0.4375, 0.0625)


def rows_weight(list_rows, rho, group_rows):
    rows = lax.broadcasted_iota(jnp.int32, (group_rows, list_rows.shape[0]), 0)
    return jnp.sum(jnp.where(rows == list_rows[None, :], rho[None, :], 0.0), axis=1)


def weights_kernel(obs_ref, row_ref, extra_ref, out_ref, flat, turned, left, held, cb, xb, wb, drive):
    blocks, _, size_k = obs_ref.shape
    dev_rows = flat.shape[0] // blocks
    tiles = size_k // TILE

    @pl.when(pl.program_id(0) == 0)
    def _():
        @pl.loop(0, blocks)
        def _(i):
            part = obs_ref[i, :dev_rows, :]
            at = pl.ds(pl.multiple_of(i * dev_rows, dev_rows), dev_rows)
            flat[at, :] = part
            turned[:, at] = part.T

    @pl.loop(0, blocks)
    def _(i):
        at = pl.ds(pl.multiple_of(i * dev_rows, dev_rows), dev_rows)
        left[:size_k, at] = (turned[:, at].astype(jnp.float32) * row_ref[0, :, at]).astype(jnp.bfloat16)

    left[size_k:, :] = extra_ref[0]

    def columns(c):
        return pl.ds(pl.multiple_of(c * TILE, TILE), TILE)

    def diagonal(c):
        row = lax.broadcasted_iota(jnp.int32, (size_k, TILE), 0)
        col = lax.broadcasted_iota(jnp.int32, (size_k, TILE), 1) + c * TILE
        return row == col

    def gram_tile(c, square):
        at = columns(c)
        both = jnp.dot(left[...], flat[:, at], preferred_element_type=jnp.float32)
        system = jnp.where(diagonal(c), 1.0, 0.0) + both[:size_k] * (1.0 / (size_k - 1))
        held[:, at] = system
        drive[0:1, at] = both[size_k : size_k + 1] + both[size_k + 1 : size_k + 2]
        return square + jnp.sum(system * system, axis=0, keepdims=True)

    square = lax.fori_loop(0, tiles, gram_tile, jnp.zeros((1, TILE), jnp.float32))
    total = jnp.sum(square, axis=1, keepdims=True)
    norm_scale = 2.0 * jnp.sqrt(total / size_k + 1e-06)
    inv_norm = 1.0 / norm_scale
    inv_root = 1.0 / jnp.sqrt(norm_scale)

    @pl.loop(0, tiles)
    def _(c):
        at = columns(c)
        centred = held[:, at] * inv_norm - jnp.where(diagonal(c), 0.5, 0.0)
        held[:, at] = centred
        cb[:, at] = centred.astype(jnp.bfloat16)

    @pl.loop(0, tiles)
    def _(c):
        at = columns(c)
        second = jnp.dot(cb[...], cb[:, at], preferred_element_type=jnp.float32)
        first = held[:, at]
        xb[:, at] = second.astype(jnp.bfloat16)
        wb[:, at] = (POLY[4] * second + POLY[3] * first).astype(jnp.bfloat16)
        held[:, at] = jnp.where(diagonal(c), POLY[0], 0.0) + POLY[1] * first + POLY[2] * second

    def root_tile(c, acc):
        at = columns(c)
        high = jnp.dot(xb[...], wb[:, at], preferred_element_type=jnp.float32)
        root = (held[:, at] + high) * inv_root
        held[:, at] = root
        return acc + jnp.sum(root * drive[0:1, at], axis=1, keepdims=True)

    inner = lax.fori_loop(0, tiles, root_tile, jnp.zeros((size_k, 1), jnp.float32))

    @pl.loop(0, tiles)
    def _(c):
        at = columns(c)
        root = held[:, at]
        mean_weight = jnp.sum(root * inner, axis=0, keepdims=True) * (1.0 / (size_k - 1))
        out_ref[0, :, at] = (root + mean_weight).astype(jnp.bfloat16)


def three_weights(gathered, row_weight, extra, dev_rows):
    blocks, aug_rows, size_k = gathered.shape
    rows = blocks * dev_rows
    flops = 3 * 2 * size_k * size_k * (rows + 2 * size_k)
    return pl.pallas_call(
        weights_kernel,
        grid=(3,),
        out_shape=jax.ShapeDtypeStruct((3, size_k, size_k), jnp.bfloat16),
        in_specs=[
            pl.BlockSpec((blocks, aug_rows, size_k), lambda t: (0, 0, 0), pipeline_mode=pl.Buffered(1)),
            pl.BlockSpec((1, 1, rows), lambda t: (t, 0, 0)),
            pl.BlockSpec((1, EXTRA, rows), lambda t: (t, 0, 0)),
        ],
        out_specs=pl.BlockSpec((1, size_k, size_k), lambda t: (t, 0, 0)),
        scratch_shapes=[
            pltpu.VMEM((rows, size_k), jnp.bfloat16),
            pltpu.VMEM((size_k, rows), jnp.bfloat16),
            pltpu.VMEM((size_k + EXTRA, rows), jnp.bfloat16),
            pltpu.VMEM((size_k, size_k), jnp.float32),
            pltpu.VMEM((size_k, size_k), jnp.bfloat16),
            pltpu.VMEM((size_k, size_k), jnp.bfloat16),
            pltpu.VMEM((size_k, size_k), jnp.bfloat16),
            pltpu.VMEM((8, size_k), jnp.float32),
        ],
        compiler_params=pltpu.CompilerParams(vmem_limit_bytes=VMEM_BYTES),
        cost_estimate=pl.CostEstimate(flops=flops, bytes_accessed=12 * 1024 * 1024, transcendentals=0),
    )(gathered, row_weight, extra)


def blend_kernel(member_ref, weight_ref, share_ref, out_ref):
    values = member_ref[...].astype(jnp.float32)
    mean_field = jnp.sum(values, axis=0, keepdims=True) / values.shape[0]
    anomaly = (values - mean_field).astype(jnp.bfloat16)
    total = mean_field
    for t in range(3):
        moved = jnp.dot(weight_ref[t], anomaly, preferred_element_type=jnp.float32)
        total = total + share_ref[t : t + 1, :] * moved
    out_ref[...] = total.astype(jnp.bfloat16)


def blend(by_column, weights, shares):
    size_k, width = by_column.shape
    return pl.pallas_call(
        blend_kernel,
        grid=(width // TILE,),
        out_shape=jax.ShapeDtypeStruct(by_column.shape, jnp.bfloat16),
        in_specs=[
            pl.BlockSpec((size_k, TILE), lambda c: (0, c)),
            pl.BlockSpec(weights.shape, lambda c: (0, 0, 0), pipeline_mode=pl.Buffered(1)),
            pl.BlockSpec((3, TILE), lambda c: (0, c)),
        ],
        out_specs=pl.BlockSpec((size_k, TILE), lambda c: (0, c)),
        compiler_params=pltpu.CompilerParams(vmem_limit_bytes=VMEM_BYTES),
        cost_estimate=pl.CostEstimate(
            flops=6 * size_k * size_k * width, bytes_accessed=14 * 1024 * 1024, transcendentals=0
        ),
    )(by_column, weights, shares)


def split(values):
    high = lax.reduce_precision(values, 8, 7)
    low = lax.reduce_precision(values - high, 8, 7)
    return high.astype(jnp.bfloat16), low.astype(jnp.bfloat16)


def gather_rows(packed):
    return lax.all_gather(packed, "sub", axis=0)


def local(
    members,
    obs_perturb,
    innovations,
    obs_list,
    obs_blocks,
    obs_precision,
    interp_slots,
    interp_weight,
):
    n_sub = lax.axis_size("sub")
    me = lax.axis_index("sub")
    dev_rows, size_k = obs_perturb.shape
    rows = n_sub * dev_rows
    inside = jnp.arange(obs_list.shape[1], dtype=jnp.int32) < obs_blocks[0] * BLOCK
    rho = jnp.where(inside, obs_precision[0], jnp.float32(0.0))
    high, low = split(rows_weight(obs_list[0], rho, rows))
    tail = jnp.concatenate([high, low, innovations])
    tail = jnp.pad(tail, (0, EXTRA * size_k - tail.shape[0])).reshape(EXTRA, size_k)
    gathered = gather_rows(jnp.concatenate([obs_perturb, tail], axis=0))
    by_column = lax.all_to_all(members, ("region", "sub"), split_axis=1, concat_axis=0, tiled=True)

    tails = gathered[:, dev_rows:, :].reshape(n_sub, EXTRA * size_k)
    innov = tails[:, 2 * rows : 2 * rows + dev_rows].reshape(rows).astype(jnp.float32)
    near = jnp.stack(
        [lax.dynamic_index_in_dim(tails, lax.rem(me + s, n_sub), 0, False) for s in (n_sub - 1, 0, 1)]
    ).astype(jnp.float32)
    weight = near[:, :rows] + near[:, rows : 2 * rows]
    extra = jnp.stack(split(weight * innov[None, :]), axis=1)
    extra = jnp.pad(extra, ((0, 0), (0, EXTRA - 2), (0, 0)))
    weights = three_weights(gathered, weight[:, None, :], extra, dev_rows)

    slots = jnp.arange(3, dtype=jnp.int32)[:, None]
    share = jnp.where(interp_slots[None, :, 0] == slots, interp_weight[None], 0.0) + jnp.where(
        interp_slots[None, :, 1] == slots, 1.0 - interp_weight[None], 0.0
    )
    return blend(by_column, weights, jnp.repeat(share, LEV * VARS, axis=1))


def solution(mesh):
    in_specs = (
        P(("region", "sub"), None),
        P(("region", "sub"), None),
        P(("region", "sub")),
        P(("region", "sub"), None),
        P(("region", "sub")),
        P(("region", "sub"), None),
        P(("region", "sub"), None),
        P(("region", "sub")),
    )
    out_specs = P(None, ("region", "sub"))
    return jax.shard_map(local, mesh=mesh, in_specs=in_specs, out_specs=out_specs, check_vma=False)
```

profile of v0, /device:TPU:0, one launch (start us, length us, event | category | flops | bytes accessed | tf_op | source)
XLA Modules:
  0.0 171.1 jit_solution(8846330537690734509)
XLA Ops:
  6.5 0.0 all-gather.3.cloned.1.call-start
  7.2 0.7 compare_select_fusion
  7.9 2.4 %select_reduce_fusion = f32[2048]{0:T(1024)S(1)} fusion(f32[2048]{0:T(1024)S(1)} %bitcast.33, s32[2048]{0:T(1024)} %bitcast.34), kind=kLoop, calls=%fused_computation | loop fusion | flops 12580864 | bytes 24576 | tf_op jit(solution)/shard_map/reduce_sum | solution.py:19
  10.4 0.7 fusion.9
  11.0 1.9 %pad_maximum_fusion = bf16[272,1024]{1,0:T(8,128)(2,1)} fusion(bf16[16,1024]{1,0:T(8,128)(2,1)S(1)} %reshape.34, bf16[256,1024]{1,0:T(8,128)(2,1)} %param.9), kind=kLoop, calls=%fused_computation.3 | loop fusion | flops 1114112 | bytes 1114112 | tf_op jit(solution)/shard_map/concatenate | solution.py:186
  12.9 0.0 all-gather.3.cloned.1.call-update
  13.0 4.8 %copy.25 = bf16[4,32,8,2048]{3,2,0,1:T(8,128)(2,1)} copy(bf16[4,32,8,2048]{3,2,1,0:T(8,128)(2,1)} %bitcast.26) | data formatting | bytes 8388608 | tf_op jit(solution)/shard_map/all_to_all | solution.py:187
  17.7 0.0 copy-start.1
  17.7 0.0 copy-start
  17.8 7.4 %all-to-all-start = ((bf16[32,32,2048]{2,0,1:T(8,128)(2,1)}), bf16[32,32,2048]{2,0,1:T(8,128)(2,1)}, u32[]{:S(2)}, u32[]{:S(2)}) async-start(bf16[32,32,2048]{2,0,1:T(8,128)(2,1)} %bitcast.25), calls=%async_computation | async-start | bytes 8388608 | tf_op jit(solution)/shard_map/all_to_all | solution.py:187
  25.2 0.0 copy-done.1
  25.2 0.0 copy-done
  25.3 0.1 broadcast_in_dim.55
  25.3 0.7 reshape.36.share_ref
  26.1 65.1 %all-gather.3.cloned.1.call-done = bf16[2176,1024]{1,0:T(8,128)(2,1)} async-done(((bf16[272,1024]{1,0:T(8,128)(2,1)}), bf16[2176,1024]{1,0:T(8,128)(2,1)}) %all-gather.3.cloned.1.call-update) | async-done | bytes 4456464 | tf_op jit(solution)/shard_map/all_gather | solution.py:164
  91.1 1.0 slice_bitcast_fusion
  92.1 0.2 copy.22
  92.3 0.2 constant_dynamic-slice_fusion.2
  92.5 0.1 fusion.11
  92.6 0.6 broadcast_in_dim.51.row_ref
  93.3 0.7 fusion.2.extra_ref
  94.0 50.2 %shard_map.82.weight_ref = bf16[3,1024,1024]{2,1,0:T(8,128)(2,1)} custom-call(bf16[8,272,1024]{2,1,0:T(8,128)(2,1)} %bitcast.32, f32[3,1,2048]{2,1,0:T(1,128)} %broadcast_in_dim.51.row_ref, bf16[3,16,2048]{2,1,0:T(8,128)(2,1)} %fusion.2.extra_ref), custom_call_target="tpu_custom_call" | custom-call | flops 25769803776 | bytes 12582912 | tf_op jit(solution)/shard_map/pallas_call | solution.py:102
  144.2 0.0 all-to-all-done
  144.2 20.0 %shard_map.83 = bf16[1024,2048]{1,0:T(8,128)(2,1)} custom-call(bf16[1024,2048]{1,0:T(8,128)(2,1)} %bitcast.1.member_ref, bf16[3,1024,1024]{2,1,0:T(8,128)(2,1)} %shard_map.82.weight_ref, f32[3,2048]{1,0:T(4,128)} %reshape.36.share_ref), custom_call_target="tpu_custom_call" | custom-call | flops 12884901888 | bytes 14680064 | tf_op jit(solution)/shard_map/pallas_call | solution.py:140
  (10 shorter events, 0.1 us)
Async XLA Ops:
  6.5 84.6 %all-gather.3.cloned.1.call-start = ((), (), s32[]{:S(2)}) async-start(), calls=%async_computation.1 | async-start | bytes 5013504 | tf_op jit(solution)/shard_map/all_gather | solution.py:164
  17.7 7.5 %copy-start.1 = (f32[64]{0:T(128)S(1)}, f32[64]{0:T(128)}, u32[]{:S(2)}) copy-start(f32[64]{0:T(128)} %param.15) | copy-start | bytes 772
  17.7 7.5 %copy-start = (s32[64,2]{0,1:T(2,128)S(1)}, s32[64,2]{0,1:T(2,128)}, u32[]{:S(2)}) copy-start(s32[64,2]{0,1:T(2,128)} %param.14) | copy-start | bytes 1540
  17.8 126.5 %all-to-all-start = ((bf16[32,32,2048]{2,0,1:T(8,128)(2,1)}), bf16[32,32,2048]{2,0,1:T(8,128)(2,1)}, u32[]{:S(2)}, u32[]{:S(2)}) async-start(bf16[32,32,2048]{2,0,1:T(8,128)(2,1)} %bitcast.25), calls=%async_computation | async-start | bytes 8388608 | tf_op jit(solution)/shard_map/all_to_all | solution.py:187
Sparse Core Ops, SparseCore 0:
  13.1 77.9 all-gather.2
where the time goes:
time: 173 us; the launch traced here: 171 us
  Pallas kernels  70.2 us (41%)
  waiting for transfers between devices  65.1 us (38%)
  between operations  14.2 us (8%)
  local copies, waits for them, and re-layouts  7.63 us (4%)
  starting transfers between devices  7.43 us (4%)
  other arithmetic  6.55 us (4%)
    all_gather x1, waiting for transfers between devices, gather_rows(): return lax.all_gather(packed, 'sub', axis=0)  65.1 us
    pallas_call x1, Pallas kernels, three_weights(): pl.pallas_call(weights_kernel, grid=(3,), out_shape=jax.ShapeDtypeStruct(...  50.2 us
    pallas_call x1, Pallas kernels, blend(): pl.pallas_call(blend_kernel, grid=(width // TILE,), out_shape=jax.ShapeDt...  20 us
    all_to_all x1, starting transfers between devices, local(): lax.all_to_all(members, ('region', 'sub'), split_axis=1, concat_axis=0, t...  7.43 us
    all_to_all x1, local copies, waits for them, and re-layouts, local(): lax.all_to_all(members, ('region', 'sub'), split_axis=1, concat_axis=0, t...  4.79 us
  transfers between devices with their start and end apart: 2, of which 1 were waited for; matrix products, arithmetic and copies ran while one was open for 5% of the time, Pallas kernels for 29%

commit v1 on v0

--- a/solution.py
+++ b/solution.py
@@ -1,3 +1,5 @@
+import functools
+
 import jax
 import jax.numpy as jnp
 from jax import lax
@@ -19,7 +21,7 @@
     return jnp.sum(jnp.where(rows == list_rows[None, :], rho[None, :], 0.0), axis=1)
 
 
-def weights_kernel(obs_ref, row_ref, extra_ref, out_ref, flat, turned, left, held, cb, xb, wb, drive):
+def weights_kernel(obs_ref, row_ref, extra_ref, out_ref, sum_ref, flat, turned, left, held, cb, xb, wb, drive):
     blocks, _, size_k = obs_ref.shape
     dev_rows = flat.shape[0] // blocks
     tiles = size_k // TILE
@@ -87,12 +89,15 @@
 
     inner = lax.fori_loop(0, tiles, root_tile, jnp.zeros((size_k, 1), jnp.float32))
 
-    @pl.loop(0, tiles)
-    def _(c):
+    def final_tile(c, acc):
         at = columns(c)
         root = held[:, at]
         mean_weight = jnp.sum(root * inner, axis=0, keepdims=True) * (1.0 / (size_k - 1))
-        out_ref[0, :, at] = (root + mean_weight).astype(jnp.bfloat16)
+        rounded = (root + mean_weight).astype(jnp.bfloat16)
+        out_ref[0, :, at] = rounded
+        return acc + jnp.sum(rounded.astype(jnp.float32), axis=1, keepdims=True)
+
+    sum_ref[0] = lax.fori_loop(0, tiles, final_tile, jnp.zeros((size_k, 1), jnp.float32))
 
 
 def three_weights(gathered, row_weight, extra, dev_rows):
@@ -102,13 +107,19 @@
     return pl.pallas_call(
         weights_kernel,
         grid=(3,),
-        out_shape=jax.ShapeDtypeStruct((3, size_k, size_k), jnp.bfloat16),
+        out_shape=(
+            jax.ShapeDtypeStruct((3, size_k, size_k), jnp.bfloat16),
+            jax.ShapeDtypeStruct((3, size_k, 1), jnp.float32),
+        ),
         in_specs=[
             pl.BlockSpec((blocks, aug_rows, size_k), lambda t: (0, 0, 0), pipeline_mode=pl.Buffered(1)),
             pl.BlockSpec((1, 1, rows), lambda t: (t, 0, 0)),
             pl.BlockSpec((1, EXTRA, rows), lambda t: (t, 0, 0)),
         ],
-        out_specs=pl.BlockSpec((1, size_k, size_k), lambda t: (t, 0, 0)),
+        out_specs=(
+            pl.BlockSpec((1, size_k, size_k), lambda t: (t, 0, 0)),
+            pl.BlockSpec((1, size_k, 1), lambda t: (t, 0, 0)),
+        ),
         scratch_shapes=[
             pltpu.VMEM((rows, size_k), jnp.bfloat16),
             pltpu.VMEM((size_k, rows), jnp.bfloat16),
@@ -124,18 +135,17 @@
     )(gathered, row_weight, extra)
 
 
-def blend_kernel(member_ref, weight_ref, share_ref, out_ref):
-    values = member_ref[...].astype(jnp.float32)
-    mean_field = jnp.sum(values, axis=0, keepdims=True) / values.shape[0]
-    anomaly = (values - mean_field).astype(jnp.bfloat16)
+def blend_kernel(member_ref, weight_ref, sum_ref, share_ref, out_ref):
+    values = member_ref[...]
+    mean_field = jnp.sum(values.astype(jnp.float32), axis=0, keepdims=True) / values.shape[0]
     total = mean_field
     for t in range(3):
-        moved = jnp.dot(weight_ref[t], anomaly, preferred_element_type=jnp.float32)
-        total = total + share_ref[t : t + 1, :] * moved
+        moved = jnp.dot(weight_ref[t], values, preferred_element_type=jnp.float32)
+        total = total + share_ref[t : t + 1, :] * (moved - sum_ref[t] * mean_field)
     out_ref[...] = total.astype(jnp.bfloat16)
 
 
-def blend(by_column, weights, shares):
+def blend(by_column, weights, sums, shares):
     size_k, width = by_column.shape
     return pl.pallas_call(
         blend_kernel,
@@ -144,6 +154,7 @@
         in_specs=[
             pl.BlockSpec((size_k, TILE), lambda c: (0, c)),
             pl.BlockSpec(weights.shape, lambda c: (0, 0, 0), pipeline_mode=pl.Buffered(1)),
+            pl.BlockSpec(sums.shape, lambda c: (0, 0, 0), pipeline_mode=pl.Buffered(1)),
             pl.BlockSpec((3, TILE), lambda c: (0, c)),
         ],
         out_specs=pl.BlockSpec((size_k, TILE), lambda c: (0, c)),
@@ -151,7 +162,7 @@
         cost_estimate=pl.CostEstimate(
             flops=6 * size_k * size_k * width, bytes_accessed=14 * 1024 * 1024, transcendentals=0
         ),
-    )(by_column, weights, shares)
+    )(by_column, weights, sums, shares)
 
 
 def split(values):
@@ -160,8 +171,61 @@
     return high.astype(jnp.bfloat16), low.astype(jnp.bfloat16)
 
 
+def gather_kernel(half, src, dst, out_send, out_recv, pair_send, pair_recv, own):
+    me = lax.axis_index("sub")
+    core, chip = lax.rem(me, 2), me // 2
+    partner = me + 1 - 2 * core
+
+    def same(offset):
+        return 2 * lax.rem(chip + offset, half) + core
+
+    def remote(source, slot, send, recv, target):
+        return pltpu.make_async_remote_copy(
+            src_ref=source,
+            dst_ref=dst.at[slot],
+            send_sem=send,
+            recv_sem=recv,
+            device_id={"sub": target},
+            device_id_type=pl.DeviceIdType.MESH,
+        )
+
+    barrier = pltpu.get_barrier_semaphore()
+    for target in [partner] + [same(i) for i in range(1, half)]:
+        pl.semaphore_signal(barrier, inc=1, device_id={"sub": target}, device_id_type=pl.DeviceIdType.MESH)
+    pl.semaphore_wait(barrier, half)
+
+    outward = []
+    for i in range(1, half):
+        outward.append(remote(src, me, out_send.at[i], out_recv.at[i], same(i)))
+        outward[-1].start()
+    across = [remote(src, me, pair_send.at[0], pair_recv.at[0], partner)]
+    across[0].start()
+    kept = pltpu.make_async_copy(src, dst.at[me], own)
+    kept.start()
+    for i in range(1, half):
+        outward[i - 1].wait_recv()
+        owner = same(half - i)
+        across.append(remote(dst.at[owner], owner, pair_send.at[i], pair_recv.at[i], partner))
+        across[-1].start()
+    kept.wait()
+    for copy in outward:
+        copy.wait_send()
+    for copy in across:
+        copy.wait()
+
+
 def gather_rows(packed):
-    return lax.all_gather(packed, "sub", axis=0)
+    size = lax.axis_size("sub")
+    half = size // 2
+    return pl.pallas_call(
+        functools.partial(gather_kernel, half),
+        out_shape=jax.ShapeDtypeStruct((size,) + packed.shape, packed.dtype),
+        in_specs=[pl.BlockSpec(memory_space=pl.ANY)],
+        out_specs=pl.BlockSpec(memory_space=pl.ANY),
+        scratch_shapes=[pltpu.SemaphoreType.DMA((half,))] * 4 + [pltpu.SemaphoreType.DMA],
+        compiler_params=pltpu.CompilerParams(collective_id=0, has_side_effects=True),
+        cost_estimate=pl.CostEstimate(flops=0, bytes_accessed=64 * 1024 * 1024, transcendentals=0),
+    )(packed)
 
 
 def local(
@@ -194,13 +258,13 @@
     weight = near[:, :rows] + near[:, rows : 2 * rows]
     extra = jnp.stack(split(weight * innov[None, :]), axis=1)
     extra = jnp.pad(extra, ((0, 0), (0, EXTRA - 2), (0, 0)))
-    weights = three_weights(gathered, weight[:, None, :], extra, dev_rows)
+    weights, sums = three_weights(gathered, weight[:, None, :], extra, dev_rows)
 
     slots = jnp.arange(3, dtype=jnp.int32)[:, None]
     share = jnp.where(interp_slots[None, :, 0] == slots, interp_weight[None], 0.0) + jnp.where(
         interp_slots[None, :, 1] == slots, 1.0 - interp_weight[None], 0.0
     )
-    return blend(by_column, weights, jnp.repeat(share, LEV * VARS, axis=1))
+    return blend(by_column, weights, sums, jnp.repeat(share, LEV * VARS, axis=1))
 
 
 def solution(mesh):

time: 173 us -> 165 us (0.954)
  the two profiles are of different devices: /device:TPU:0 before, /device:TPU:21 now
where the time goes in v1:
time: 165 us; the launch traced here: 164 us
  Pallas kernels  146 us (88%)
  local copies, waits for them, and re-layouts  7.66 us (5%)
  starting transfers between devices  6.27 us (4%)
  other arithmetic  3.47 us (2%)
    pallas_call x1, Pallas kernels, gather_rows(): pl.pallas_call(functools.partial(gather_kernel, half), out_shape=jax.Shap...  73.5 us
    pallas_call x1, Pallas kernels, three_weights(): pl.pallas_call(weights_kernel, grid=(3,), out_shape=(jax.ShapeDtypeStruct...  52.7 us
    pallas_call x1, Pallas kernels, blend(): pl.pallas_call(blend_kernel, grid=(width // TILE,), out_shape=jax.ShapeDt...  20 us
    all_to_all x1, starting transfers between devices, local(): lax.all_to_all(members, ('region', 'sub'), split_axis=1, concat_axis=0, t...  6.27 us
    all_to_all x1, local copies, waits for them, and re-layouts, local(): lax.all_to_all(members, ('region', 'sub'), split_axis=1, concat_axis=0, t...  4.79 us
  transfers between devices with their start and end apart: 1, of which 0 were waited for; matrix products, arithmetic and copies ran while one was open for 4% of the time, Pallas kernels for 77%

profile of v1, /device:TPU:21, one launch (start us, length us, event | category | flops | bytes accessed | tf_op | source)
XLA Modules:
  0.0 164.5 jit_solution(16693692617677367683)
XLA Ops:
  0.0 4.8 %copy.25 = bf16[4,32,8,2048]{3,2,0,1:T(8,128)(2,1)} copy(bf16[4,32,8,2048]{3,2,1,0:T(8,128)(2,1)} %bitcast.25) | data formatting | bytes 8388608 | tf_op jit(solution)/shard_map/all_to_all | solution.py:251
  4.8 0.0 copy-start.1
  4.8 0.0 copy-start.5
  4.8 0.0 copy-start.4
  4.8 0.0 copy-start.3
  4.8 0.0 copy-start.2
  4.8 0.0 copy-start
  4.8 6.3 %all-to-all-start = ((bf16[32,32,2048]{2,0,1:T(8,128)(2,1)}), bf16[32,32,2048]{2,0,1:T(8,128)(2,1)}, u32[]{:S(2)}, u32[]{:S(2)}) async-start(bf16[32,32,2048]{2,0,1:T(8,128)(2,1)} %bitcast.24), calls=%async_computation | async-start | bytes 8388608 | tf_op jit(solution)/shard_map/all_to_all | solution.py:251
  11.8 0.0 copy-done.1
  11.8 0.0 copy-done.5
  11.8 1.7 %select_reduce_fusion = f32[2048]{0:T(1024)S(1)} fusion(f32[2048]{0:T(1024)S(1)} %bitcast.30, s32[2048]{0:T(1024)S(1)} %bitcast.31), kind=kLoop, calls=%fused_computation | loop fusion | flops 12580864 | bytes 24576 | tf_op jit(solution)/shard_map/reduce_sum | solution.py:21
  13.6 0.0 copy-done.4
  13.6 0.0 copy-done.3
  13.6 0.0 copy-done.2
  13.7 0.1 broadcast_in_dim.55
  13.8 0.7 reshape.36.share_ref
  14.5 0.0 copy-done
  14.5 0.8 pad_maximum_fusion.src
  15.3 73.5 %shard_map.82.obs_ref = bf16[8,272,1024]{2,1,0:T(8,128)(2,1)} custom-call(bf16[272,1024]{1,0:T(8,128)(2,1)} %pad_maximum_fusion.src), custom_call_target="tpu_custom_call" | custom-call | bytes 67108864 | tf_op jit(solution)/shard_map/pallas_call | solution.py:220
  88.8 1.0 slice_bitcast_fusion
  89.8 0.2 copy.22
  90.0 0.2 constant_dynamic-slice_fusion.2
  90.2 0.1 fusion.11
  90.3 0.6 broadcast_in_dim.51.row_ref
  91.0 0.8 fusion.2.extra_ref
  91.8 52.7 %shard_map.83 = (bf16[3,1024,1024]{2,1,0:T(8,128)(2,1)}, f32[3,1024,1]{2,1,0:T(8,128)}) custom-call(bf16[8,272,1024]{2,1,0:T(8,128)(2,1)} %shard_map.82.obs_ref, f32[3,1,2048]{2,1,0:T(1,128)} %broadcast_in_dim.51.row_ref, bf16[3,16,2048]{2,1,0:T(8,128)(2,1)} %fusion.2.extra_ref), custom_call_target="tpu_custom_call" | custom-call | flops 25769803776 | bytes 12582912 | tf_op jit(solution)/shard_map/pallas_call | solution.py:107
  144.5 0.0 all-to-all-done
  144.5 20.0 %shard_map.84 = bf16[1024,2048]{1,0:T(8,128)(2,1)} custom-call(bf16[1024,2048]{1,0:T(8,128)(2,1)} %bitcast.1.member_ref, bf16[3,1024,1024]{2,1,0:T(8,128)(2,1)} %get-tuple-element.7.weight_ref, f32[3,1024,1]{2,1,0:T(8,128)} %get-tuple-element.8.sum_ref, f32[3,2048]{1,0:T(4,128)} %reshape.36.share_ref), custom_call_target="tpu_custom_call" | custom-call | flops 12884901888 | bytes 14680064 | tf_op jit(solution)/shard_map/pallas_call | solution.py:150
  (12 shorter events, 0.1 us)
Async XLA Ops:
  4.8 7.0 %copy-start.1 = (f32[1,2048]{1,0:T(1,128)S(1)}, f32[1,2048]{1,0:T(1,128)}, u32[]{:S(2)}) copy-start(f32[1,2048]{1,0:T(1,128)} %param.13) | copy-start | bytes 24580
  4.8 7.0 %copy-start.5 = (s32[1,2048]{1,0:T(1,128)S(1)}, s32[1,2048]{1,0:T(1,128)}, u32[]{:S(2)}) copy-start(s32[1,2048]{1,0:T(1,128)} %param.11) | copy-start | bytes 24580
  4.8 8.8 %copy-start.4 = (bf16[256]{0:T(256)(128)(2,1)S(1)}, bf16[256]{0:T(256)(128)(2,1)}, u32[]{:S(2)}) copy-start(bf16[256]{0:T(256)(128)(2,1)} %param.10) | copy-start | bytes 1540
  4.8 8.8 %copy-start.3 = (f32[64]{0:T(128)S(1)}, f32[64]{0:T(128)}, u32[]{:S(2)}) copy-start(f32[64]{0:T(128)} %param.15) | copy-start | bytes 772
  4.8 8.8 %copy-start.2 = (s32[64,2]{0,1:T(2,128)S(1)}, s32[64,2]{0,1:T(2,128)}, u32[]{:S(2)}) copy-start(s32[64,2]{0,1:T(2,128)} %param.14) | copy-start | bytes 1540
  4.8 9.7 %copy-start = (bf16[256,1024]{1,0:T(8,128)(2,1)S(1)}, bf16[256,1024]{1,0:T(8,128)(2,1)}, u32[]{:S(2)}) copy-start(bf16[256,1024]{1,0:T(8,128)(2,1)} %param.9) | copy-start | bytes 1572868
  4.8 139.7 %all-to-all-start = ((bf16[32,32,2048]{2,0,1:T(8,128)(2,1)}), bf16[32,32,2048]{2,0,1:T(8,128)(2,1)}, u32[]{:S(2)}, u32[]{:S(2)}) async-start(bf16[32,32,2048]{2,0,1:T(8,128)(2,1)} %bitcast.24), calls=%async_computation | async-start | bytes 8388608 | tf_op jit(solution)/shard_map/all_to_all | solution.py:251

commit v2 on v1

--- a/solution.py
+++ b/solution.py
@@ -12,6 +12,7 @@
 BLOCK = 128
 EXTRA = 16
 TILE = 256
+BLEND_TILE = 512
 VMEM_BYTES = 60 * 1024 * 1024
 POLY = (1.38671875, -1.140625, 0.9375, -0.4375, 0.0625)
 
@@ -21,7 +22,7 @@
     return jnp.sum(jnp.where(rows == list_rows[None, :], rho[None, :], 0.0), axis=1)
 
 
-def weights_kernel(obs_ref, row_ref, extra_ref, out_ref, sum_ref, flat, turned, left, held, cb, xb, wb, drive):
+def weights_kernel(obs_ref, row_ref, extra_ref, out_ref, flat, turned, left, held, cb, xb, wb, drive):
     blocks, _, size_k = obs_ref.shape
     dev_rows = flat.shape[0] // blocks
     tiles = size_k // TILE
@@ -89,15 +90,12 @@
 
     inner = lax.fori_loop(0, tiles, root_tile, jnp.zeros((size_k, 1), jnp.float32))
 
-    def final_tile(c, acc):
+    @pl.loop(0, tiles)
+    def _(c):
         at = columns(c)
         root = held[:, at]
         mean_weight = jnp.sum(root * inner, axis=0, keepdims=True) * (1.0 / (size_k - 1))
-        rounded = (root + mean_weight).astype(jnp.bfloat16)
-        out_ref[0, :, at] = rounded
-        return acc + jnp.sum(rounded.astype(jnp.float32), axis=1, keepdims=True)
-
-    sum_ref[0] = lax.fori_loop(0, tiles, final_tile, jnp.zeros((size_k, 1), jnp.float32))
+        out_ref[:, at] = (root + mean_weight).astype(jnp.bfloat16)
 
 
 def three_weights(gathered, row_weight, extra, dev_rows):
@@ -107,19 +105,13 @@
     return pl.pallas_call(
         weights_kernel,
         grid=(3,),
-        out_shape=(
-            jax.ShapeDtypeStruct((3, size_k, size_k), jnp.bfloat16),
-            jax.ShapeDtypeStruct((3, size_k, 1), jnp.float32),
-        ),
+        out_shape=jax.ShapeDtypeStruct((size_k, 3 * size_k), jnp.bfloat16),
         in_specs=[
             pl.BlockSpec((blocks, aug_rows, size_k), lambda t: (0, 0, 0), pipeline_mode=pl.Buffered(1)),
             pl.BlockSpec((1, 1, rows), lambda t: (t, 0, 0)),
             pl.BlockSpec((1, EXTRA, rows), lambda t: (t, 0, 0)),
         ],
-        out_specs=(
-            pl.BlockSpec((1, size_k, size_k), lambda t: (t, 0, 0)),
-            pl.BlockSpec((1, size_k, 1), lambda t: (t, 0, 0)),
-        ),
+        out_specs=pl.BlockSpec((size_k, size_k), lambda t: (0, t)),
         scratch_shapes=[
             pltpu.VMEM((rows, size_k), jnp.bfloat16),
             pltpu.VMEM((size_k, rows), jnp.bfloat16),
@@ -135,34 +127,35 @@
     )(gathered, row_weight, extra)
 
 
-def blend_kernel(member_ref, weight_ref, sum_ref, share_ref, out_ref):
-    values = member_ref[...]
-    mean_field = jnp.sum(values.astype(jnp.float32), axis=0, keepdims=True) / values.shape[0]
-    total = mean_field
+def blend_kernel(member_ref, weight_ref, share_ref, out_ref, shared):
+    values = member_ref[...].astype(jnp.float32)
+    size_k = values.shape[0]
+    mean_field = jnp.sum(values, axis=0, keepdims=True) / size_k
+    anomaly = values - mean_field
     for t in range(3):
-        moved = jnp.dot(weight_ref[t], values, preferred_element_type=jnp.float32)
-        total = total + share_ref[t : t + 1, :] * (moved - sum_ref[t] * mean_field)
-    out_ref[...] = total.astype(jnp.bfloat16)
-
-
-def blend(by_column, weights, sums, shares):
+        shared[t * size_k : (t + 1) * size_k, :] = (anomaly * share_ref[t : t + 1, :]).astype(jnp.bfloat16)
+    moved = jnp.dot(weight_ref[...], shared[...], preferred_element_type=jnp.float32)
+    out_ref[...] = (moved + mean_field).astype(jnp.bfloat16)
+
+
+def blend(by_column, weights, shares):
     size_k, width = by_column.shape
     return pl.pallas_call(
         blend_kernel,
-        grid=(width // TILE,),
+        grid=(width // BLEND_TILE,),
         out_shape=jax.ShapeDtypeStruct(by_column.shape, jnp.bfloat16),
         in_specs=[
-            pl.BlockSpec((size_k, TILE), lambda c: (0, c)),
-            pl.BlockSpec(weights.shape, lambda c: (0, 0, 0), pipeline_mode=pl.Buffered(1)),
-            pl.BlockSpec(sums.shape, lambda c: (0, 0, 0), pipeline_mode=pl.Buffered(1)),
-            pl.BlockSpec((3, TILE), lambda c: (0, c)),
+            pl.BlockSpec((size_k, BLEND_TILE), lambda c: (0, c)),
+            pl.BlockSpec(weights.shape, lambda c: (0, 0), pipeline_mode=pl.Buffered(1)),
+            pl.BlockSpec((3, BLEND_TILE), lambda c: (0, c)),
         ],
-        out_specs=pl.BlockSpec((size_k, TILE), lambda c: (0, c)),
+        out_specs=pl.BlockSpec((size_k, BLEND_TILE), lambda c: (0, c)),
+        scratch_shapes=[pltpu.VMEM((3 * size_k, BLEND_TILE), jnp.bfloat16)],
         compiler_params=pltpu.CompilerParams(vmem_limit_bytes=VMEM_BYTES),
         cost_estimate=pl.CostEstimate(
             flops=6 * size_k * size_k * width, bytes_accessed=14 * 1024 * 1024, transcendentals=0
         ),
-    )(by_column, weights, sums, shares)
+    )(by_column, weights, shares)
 
 
 def split(values):
@@ -248,6 +241,7 @@
     tail = jnp.concatenate([high, low, innovations])
     tail = jnp.pad(tail, (0, EXTRA * size_k - tail.shape[0])).reshape(EXTRA, size_k)
     gathered = gather_rows(jnp.concatenate([obs_perturb, tail], axis=0))
+    members, gathered = lax.optimization_barrier((members, gathered))
     by_column = lax.all_to_all(members, ("region", "sub"), split_axis=1, concat_axis=0, tiled=True)
 
     tails = gathered[:, dev_rows:, :].reshape(n_sub, EXTRA * size_k)
@@ -258,13 +252,13 @@
     weight = near[:, :rows] + near[:, rows : 2 * rows]
     extra = jnp.stack(split(weight * innov[None, :]), axis=1)
     extra = jnp.pad(extra, ((0, 0), (0, EXTRA - 2), (0, 0)))
-    weights, sums = three_weights(gathered, weight[:, None, :], extra, dev_rows)
+    weights = three_weights(gathered, weight[:, None, :], extra, dev_rows)
 
     slots = jnp.arange(3, dtype=jnp.int32)[:, None]
     share = jnp.where(interp_slots[None, :, 0] == slots, interp_weight[None], 0.0) + jnp.where(
         interp_slots[None, :, 1] == slots, 1.0 - interp_weight[None], 0.0
     )
-    return blend(by_column, weights, sums, jnp.repeat(share, LEV * VARS, axis=1))
+    return blend(by_column, weights, jnp.repeat(share, LEV * VARS, axis=1))
 
 
 def solution(mesh):

time: 165 us -> 161 us (0.976)
  the two profiles are of different devices: /device:TPU:21 before, /device:TPU:0 now
where the time goes in v2:
time: 161 us
  Pallas kernels  101 us (63%)
  waiting for transfers between devices  39.8 us (25%)
  local copies, waits for them, and re-layouts  7.62 us (5%)
  other arithmetic  6.56 us (4%)
  starting transfers between devices  5.07 us (3%)
    pallas_call x1, Pallas kernels, three_weights(): pl.pallas_call(weights_kernel, grid=(3,), out_shape=jax.ShapeDtypeStruct(...  50.2 us
    all_to_all x1, waiting for transfers between devices, local(): lax.all_to_all(members, ('region', 'sub'), split_axis=1, concat_axis=0, t...  39.8 us
    pallas_call x1, Pallas kernels, gather_rows(): pl.pallas_call(functools.partial(gather_kernel, half), out_shape=jax.Shap...  32 us
    pallas_call x1, Pallas kernels, blend(): pl.pallas_call(blend_kernel, grid=(width // BLEND_TILE,), out_shape=jax.S...  18.8 us
    all_to_all x1, starting transfers between devices, local(): lax.all_to_all(members, ('region', 'sub'), split_axis=1, concat_axis=0, t...  5.07 us
    all_to_all x1, local copies, waits for them, and re-layouts, local(): lax.all_to_all(members, ('region', 'sub'), split_axis=1, concat_axis=0, t...  4.79 us
  transfers between devices with their start and end apart: 1, of which 1 were waited for; matrix products, arithmetic and copies ran while one was open for 2% of the time, Pallas kernels for 31%

profile of v2, /device:TPU:0, one launch (start us, length us, event | category | flops | bytes accessed | tf_op | source)
XLA Modules:
  0.0 160.9 jit_solution(17417205690204409325)
XLA Ops:
  0.7 0.7 compare_select_fusion
  1.4 2.4 %select_reduce_fusion = f32[2048]{0:T(1024)S(1)} fusion(f32[2048]{0:T(1024)S(1)} %bitcast.30, s32[2048]{0:T(1024)} %bitcast.31), kind=kLoop, calls=%fused_computation | loop fusion | flops 12580864 | bytes 24576 | tf_op jit(solution)/shard_map/reduce_sum | solution.py:22
  3.8 0.7 fusion.9
  4.5 1.9 %pad_maximum_fusion.src = bf16[272,1024]{1,0:T(8,128)(2,1)} fusion(bf16[16,1024]{1,0:T(8,128)(2,1)S(1)} %reshape.34, bf16[256,1024]{1,0:T(8,128)(2,1)} %param.9), kind=kLoop, calls=%fused_computation.3 | loop fusion | flops 1114112 | bytes 1114112 | tf_op jit(solution)/shard_map/concatenate | solution.py:243
  6.4 32.0 %shard_map.82.obs_ref = bf16[8,272,1024]{2,1,0:T(8,128)(2,1)} custom-call(bf16[272,1024]{1,0:T(8,128)(2,1)} %pad_maximum_fusion.src), custom_call_target="tpu_custom_call" | custom-call | bytes 67108864 | tf_op jit(solution)/shard_map/pallas_call | solution.py:213
  38.4 4.8 %copy.25 = bf16[4,32,8,2048]{3,2,0,1:T(8,128)(2,1)} copy(bf16[4,32,8,2048]{3,2,1,0:T(8,128)(2,1)} %bitcast.25) | data formatting | bytes 8388608 | tf_op jit(solution)/shard_map/all_to_all | solution.py:245
  43.2 0.0 copy-start.1
  43.2 0.0 copy-start
  43.2 5.1 %all-to-all-start = ((bf16[32,32,2048]{2,0,1:T(8,128)(2,1)}), bf16[32,32,2048]{2,0,1:T(8,128)(2,1)}, u32[]{:S(2)}, u32[]{:S(2)}) async-start(bf16[32,32,2048]{2,0,1:T(8,128)(2,1)} %bitcast.24), calls=%async_computation | async-start | bytes 8388608 | tf_op jit(solution)/shard_map/all_to_all | solution.py:245
  48.3 1.0 slice_bitcast_fusion
  49.2 0.2 copy.22
  49.4 0.2 constant_dynamic-slice_fusion.2
  49.6 0.1 fusion.11
  49.7 0.6 broadcast_in_dim.51.row_ref
  50.4 0.0 copy-done.1
  50.4 0.0 copy-done
  50.5 0.1 broadcast_in_dim.55
  50.6 0.7 reshape.36.share_ref
  51.3 0.8 fusion.2.extra_ref
  52.0 50.2 %shard_map.83.weight_ref = bf16[1024,3072]{1,0:T(8,128)(2,1)} custom-call(bf16[8,272,1024]{2,1,0:T(8,128)(2,1)} %shard_map.82.obs_ref, f32[3,1,2048]{2,1,0:T(1,128)} %broadcast_in_dim.51.row_ref, bf16[3,16,2048]{2,1,0:T(8,128)(2,1)} %fusion.2.extra_ref), custom_call_target="tpu_custom_call" | custom-call | flops 25769803776 | bytes 12582912 | tf_op jit(solution)/shard_map/pallas_call | solution.py:105
  102.3 39.8 %all-to-all-done = bf16[32,32,2048]{2,0,1:T(8,128)(2,1)} async-done(((bf16[32,32,2048]{2,0,1:T(8,128)(2,1)}), bf16[32,32,2048]{2,0,1:T(8,128)(2,1)}, u32[]{:S(2)}, u32[]{:S(2)}) %all-to-all-start) | async-done | bytes 4194336 | tf_op jit(solution)/shard_map/all_to_all | solution.py:245
  142.1 18.8 %shard_map.84 = bf16[1024,2048]{1,0:T(8,128)(2,1)} custom-call(bf16[1024,2048]{1,0:T(8,128)(2,1)} %bitcast.4.member_ref, bf16[1024,3072]{1,0:T(8,128)(2,1)} %shard_map.83.weight_ref, f32[3,2048]{1,0:T(4,128)} %reshape.36.share_ref), custom_call_target="tpu_custom_call" | custom-call | flops 12884901888 | bytes 14680064 | tf_op jit(solution)/shard_map/pallas_call | solution.py:143
  (10 shorter events, 0.1 us)
Async XLA Ops:
  43.2 7.3 %copy-start.1 = (f32[64]{0:T(128)S(1)}, f32[64]{0:T(128)}, u32[]{:S(2)}) copy-start(f32[64]{0:T(128)} %param.15) | copy-start | bytes 772
  43.2 7.3 %copy-start = (s32[64,2]{0,1:T(2,128)S(1)}, s32[64,2]{0,1:T(2,128)}, u32[]{:S(2)}) copy-start(s32[64,2]{0,1:T(2,128)} %param.14) | copy-start | bytes 1540
  43.2 99.0 %all-to-all-start = ((bf16[32,32,2048]{2,0,1:T(8,128)(2,1)}), bf16[32,32,2048]{2,0,1:T(8,128)(2,1)}, u32[]{:S(2)}, u32[]{:S(2)}) async-start(bf16[32,32,2048]{2,0,1:T(8,128)(2,1)} %bitcast.24), calls=%async_computation | async-start | bytes 8388608 | tf_op jit(solution)/shard_map/all_to_all | solution.py:245

commit v3 on v2

--- a/solution.py
+++ b/solution.py
@@ -11,7 +11,7 @@
 VARS = 4
 BLOCK = 128
 EXTRA = 16
-TILE = 256
+TILE = 512
 BLEND_TILE = 512
 VMEM_BYTES = 60 * 1024 * 1024
 POLY = (1.38671875, -1.140625, 0.9375, -0.4375, 0.0625)
@@ -22,8 +22,8 @@
     return jnp.sum(jnp.where(rows == list_rows[None, :], rho[None, :], 0.0), axis=1)
 
 
-def weights_kernel(obs_ref, row_ref, extra_ref, out_ref, flat, turned, left, held, cb, xb, wb, drive):
-    blocks, _, size_k = obs_ref.shape
+def weights_kernel(first_ref, second_ref, row_ref, extra_ref, out_ref, flat, turned, left, held, cb, xb, wb, drive):
+    blocks, half_rows, size_k = first_ref.shape
     dev_rows = flat.shape[0] // blocks
     tiles = size_k // TILE
 
@@ -31,10 +31,11 @@
     def _():
         @pl.loop(0, blocks)
         def _(i):
-            part = obs_ref[i, :dev_rows, :]
-            at = pl.ds(pl.multiple_of(i * dev_rows, dev_rows), dev_rows)
-            flat[at, :] = part
-            turned[:, at] = part.T
+            for j, ref in enumerate((first_ref, second_ref)):
+                part = ref[i, :half_rows, :]
+                at = pl.ds(pl.multiple_of(i * dev_rows + j * half_rows, half_rows), half_rows)
+                flat[at, :] = part
+                turned[:, at] = part.T
 
     @pl.loop(0, blocks)
     def _(i):
@@ -98,8 +99,8 @@
         out_ref[:, at] = (root + mean_weight).astype(jnp.bfloat16)
 
 
-def three_weights(gathered, row_weight, extra, dev_rows):
-    blocks, aug_rows, size_k = gathered.shape
+def three_weights(first, second, row_weight, extra, dev_rows):
+    blocks, _, size_k = first.shape
     rows = blocks * dev_rows
     flops = 3 * 2 * size_k * size_k * (rows + 2 * size_k)
     return pl.pallas_call(
@@ -107,7 +108,8 @@
         grid=(3,),
         out_shape=jax.ShapeDtypeStruct((size_k, 3 * size_k), jnp.bfloat16),
         in_specs=[
-            pl.BlockSpec((blocks, aug_rows, size_k), lambda t: (0, 0, 0), pipeline_mode=pl.Buffered(1)),
+            pl.BlockSpec(first.shape, lambda t: (0, 0, 0), pipeline_mode=pl.Buffered(1)),
+            pl.BlockSpec(second.shape, lambda t: (0, 0, 0), pipeline_mode=pl.Buffered(1)),
             pl.BlockSpec((1, 1, rows), lambda t: (t, 0, 0)),
             pl.BlockSpec((1, EXTRA, rows), lambda t: (t, 0, 0)),
         ],
@@ -124,7 +126,7 @@
         ],
         compiler_params=pltpu.CompilerParams(vmem_limit_bytes=VMEM_BYTES),
         cost_estimate=pl.CostEstimate(flops=flops, bytes_accessed=12 * 1024 * 1024, transcendentals=0),
-    )(gathered, row_weight, extra)
+    )(first, second, row_weight, extra)
 
 
 def blend_kernel(member_ref, weight_ref, share_ref, out_ref, shared):
@@ -207,7 +209,7 @@
         copy.wait()
 
 
-def gather_rows(packed):
+def gather_rows(packed, number):
     size = lax.axis_size("sub")
     half = size // 2
     return pl.pallas_call(
@@ -216,7 +218,7 @@
         in_specs=[pl.BlockSpec(memory_space=pl.ANY)],
         out_specs=pl.BlockSpec(memory_space=pl.ANY),
         scratch_shapes=[pltpu.SemaphoreType.DMA((half,))] * 4 + [pltpu.SemaphoreType.DMA],
-        compiler_params=pltpu.CompilerParams(collective_id=0, has_side_effects=True),
+        compiler_params=pltpu.CompilerParams(collective_id=number, has_side_effects=True),
         cost_estimate=pl.CostEstimate(flops=0, bytes_accessed=64 * 1024 * 1024, transcendentals=0),
     )(packed)
 
@@ -240,11 +242,14 @@
     high, low = split(rows_weight(obs_list[0], rho, rows))
     tail = jnp.concatenate([high, low, innovations])
     tail = jnp.pad(tail, (0, EXTRA * size_k - tail.shape[0])).reshape(EXTRA, size_k)
-    gathered = gather_rows(jnp.concatenate([obs_perturb, tail], axis=0))
-    members, gathered = lax.optimization_barrier((members, gathered))
+    half_rows = dev_rows // 2
+    first = gather_rows(obs_perturb[:half_rows], 0)
+    packed = jnp.concatenate([obs_perturb[half_rows:], tail], axis=0)
+    members, packed, first = lax.optimization_barrier((members, packed, first))
     by_column = lax.all_to_all(members, ("region", "sub"), split_axis=1, concat_axis=0, tiled=True)
 
-    tails = gathered[:, dev_rows:, :].reshape(n_sub, EXTRA * size_k)
+    second = gather_rows(packed, 1)
+    tails = second[:, half_rows:, :].reshape(n_sub, EXTRA * size_k)
     innov = tails[:, 2 * rows : 2 * rows + dev_rows].reshape(rows).astype(jnp.float32)
     near = jnp.stack(
         [lax.dynamic_index_in_dim(tails, lax.rem(me + s, n_sub), 0, False) for s in (n_sub - 1, 0, 1)]
@@ -252,7 +257,7 @@
     weight = near[:, :rows] + near[:, rows : 2 * rows]
     extra = jnp.stack(split(weight * innov[None, :]), axis=1)
     extra = jnp.pad(extra, ((0, 0), (0, EXTRA - 2), (0, 0)))
-    weights = three_weights(gathered, weight[:, None, :], extra, dev_rows)
+    weights = three_weights(first, second, weight[:, None, :], extra, dev_rows)
 
     slots = jnp.arange(3, dtype=jnp.int32)[:, None]
     share = jnp.where(interp_slots[None, :, 0] == slots, interp_weight[None], 0.0) + jnp.where(

time: 161 us -> 166 us (1.031)
  Pallas kernels: 101 us -> 145 us
  waiting for transfers between devices: 39.8 us -> 0.01 us
  local copies, waits for them, and re-layouts: 7.62 us -> 9.41 us
    pallas_call x1 -> x2, Pallas kernels: 32 us -> 78.4 us  [gather_rows(): pl.pallas_call(functools.partial(gather_kernel, half), out_shape=jax.Shap...]
    all_to_all x1, waiting for transfers between devices: 39.8 us -> 0.01 us  [local(): lax.all_to_all(members, ('region', 'sub'), split_axis=1, concat_axis=0, t...]
    pallas_call x1, Pallas kernels: 50.2 us -> 47.8 us  [three_weights(): pl.pallas_call(weights_kernel, grid=(3,), out_shape=jax.ShapeDtypeStruct(...]
    slice x0 -> x1, local copies, waits for them, and re-layouts: none -> 1.77 us  [local(): first = gather_rows(obs_perturb[:half_rows], 0)]
  transfers between devices with their start and end apart: 1 -> 1, of which waited for: 1 -> 0; matrix products, arithmetic and copies ran while one was open for 2% -> 2% of each run, Pallas kernels for 31% -> 65%
where the time goes in v3:
time: 166 us
  Pallas kernels  145 us (87%)
  local copies, waits for them, and re-layouts  9.41 us (6%)
  starting transfers between devices  5.5 us (3%)
  other arithmetic  5.39 us (3%)
    pallas_call x2, Pallas kernels, gather_rows(): pl.pallas_call(functools.partial(gather_kernel, half), out_shape=jax.Shap...  78.4 us
    pallas_call x1, Pallas kernels, three_weights(): pl.pallas_call(weights_kernel, grid=(3,), out_shape=jax.ShapeDtypeStruct(...  47.8 us
    pallas_call x1, Pallas kernels, blend(): pl.pallas_call(blend_kernel, grid=(width // BLEND_TILE,), out_shape=jax.S...  18.8 us
    all_to_all x1, starting transfers between devices, local(): lax.all_to_all(members, ('region', 'sub'), split_axis=1, concat_axis=0, t...  5.5 us
    all_to_all x1, local copies, waits for them, and re-layouts, local(): lax.all_to_all(members, ('region', 'sub'), split_axis=1, concat_axis=0, t...  4.79 us
  transfers between devices with their start and end apart: 1, of which 0 were waited for; matrix products, arithmetic and copies ran while one was open for 2% of the time, Pallas kernels for 65%

profile of v3, /device:TPU:0, one launch (start us, length us, event | category | flops | bytes accessed | tf_op | source)
XLA Modules:
  0.0 166.1 jit_solution(655002425797366617)
XLA Ops:
  0.7 0.7 compare_select_fusion
  1.4 2.4 %select_reduce_fusion = f32[2048]{0:T(1024)S(1)} fusion(f32[2048]{0:T(1024)S(1)} %bitcast.30, s32[2048]{0:T(1024)} %bitcast.31), kind=kLoop, calls=%fused_computation | loop fusion | flops 12580864 | bytes 24576 | tf_op jit(solution)/shard_map/reduce_sum | solution.py:22
  3.8 0.7 fusion.9
  4.5 1.8 %fusion.14 = (bf16[128,1024]{1,0:T(8,128)(2,1)}, bf16[128,1024]{1,0:T(8,128)(2,1)S(1)}) fusion(bf16[256,1024]{1,0:T(8,128)(2,1)} %param.9), kind=kLoop, calls=%fused_computation.39 | loop fusion | bytes 1048576 | tf_op jit(solution)/shard_map/slice | solution.py:246
  6.3 18.5 %shard_map.82.first_ref = bf16[8,128,1024]{2,1,0:T(8,128)(2,1)} custom-call(bf16[128,1024]{1,0:T(8,128)(2,1)} %get-tuple-element.13.src), custom_call_target="tpu_custom_call" | custom-call | bytes 67108864 | tf_op jit(solution)/shard_map/pallas_call | solution.py:215
  24.8 0.7 pad_maximum_fusion.src
  25.5 4.8 %copy.25 = bf16[4,32,8,2048]{3,2,0,1:T(8,128)(2,1)} copy(bf16[4,32,8,2048]{3,2,1,0:T(8,128)(2,1)} %bitcast.25) | data formatting | bytes 8388608 | tf_op jit(solution)/shard_map/all_to_all | solution.py:249
  30.3 5.5 %all-to-all-start = ((bf16[32,32,2048]{2,0,1:T(8,128)(2,1)}), bf16[32,32,2048]{2,0,1:T(8,128)(2,1)}, u32[]{:S(2)}, u32[]{:S(2)}) async-start(bf16[32,32,2048]{2,0,1:T(8,128)(2,1)} %bitcast.24), calls=%async_computation | async-start | bytes 8388608 | tf_op jit(solution)/shard_map/all_to_all | solution.py:249
  35.8 0.0 copy-start.1
  35.8 0.0 copy-start
  35.8 59.9 %shard_map.83.second_ref = bf16[8,144,1024]{2,1,0:T(8,128)(2,1)} custom-call(bf16[144,1024]{1,0:T(8,128)(2,1)} %pad_maximum_fusion.src), custom_call_target="tpu_custom_call" | custom-call | bytes 67108864 | tf_op jit(solution)/shard_map/pallas_call | solution.py:215
  95.8 1.0 slice_bitcast_fusion
  96.7 0.2 copy.22
  96.9 0.2 constant_dynamic-slice_fusion.2
  97.2 0.1 fusion.11
  97.2 0.6 broadcast_in_dim.51.row_ref
  97.9 0.0 copy-done.1
  97.9 0.0 copy-done
  98.0 0.1 broadcast_in_dim.55
  98.1 0.7 reshape.36.share_ref
  98.8 0.7 fusion.2.extra_ref
  99.6 47.8 %shard_map.84.weight_ref = bf16[1024,3072]{1,0:T(8,128)(2,1)} custom-call(bf16[8,128,1024]{2,1,0:T(8,128)(2,1)} %shard_map.82.first_ref, bf16[8,144,1024]{2,1,0:T(8,128)(2,1)} %shard_map.83.second_ref, f32[3,1,2048]{2,1,0:T(1,128)} %broadcast_in_dim.51.row_ref, bf16[3,16,2048]{2,1,0:T(8,128)(2,1)} %fusion.2.extra_ref), custom_call_target="tpu_custom_call" | custom-call | flops 25769803776 | bytes 12582912 | tf_op jit(solution)/shard_map/pallas_call | solution.py:106
  147.3 0.0 all-to-all-done
  147.4 18.8 %shard_map.85 = bf16[1024,2048]{1,0:T(8,128)(2,1)} custom-call(bf16[1024,2048]{1,0:T(8,128)(2,1)} %bitcast.4.member_ref, bf16[1024,3072]{1,0:T(8,128)(2,1)} %shard_map.84.weight_ref, f32[3,2048]{1,0:T(4,128)} %reshape.36.share_ref), custom_call_target="tpu_custom_call" | custom-call | flops 12884901888 | bytes 14680064 | tf_op jit(solution)/shard_map/pallas_call | solution.py:145
  (10 shorter events, 0.1 us)
Async XLA Ops:
  30.3 117.1 %all-to-all-start = ((bf16[32,32,2048]{2,0,1:T(8,128)(2,1)}), bf16[32,32,2048]{2,0,1:T(8,128)(2,1)}, u32[]{:S(2)}, u32[]{:S(2)}) async-start(bf16[32,32,2048]{2,0,1:T(8,128)(2,1)} %bitcast.24), calls=%async_computation | async-start | bytes 8388608 | tf_op jit(solution)/shard_map/all_to_all | solution.py:249
  35.8 62.2 %copy-start.1 = (f32[64]{0:T(128)S(1)}, f32[64]{0:T(128)}, u32[]{:S(2)}) copy-start(f32[64]{0:T(128)} %param.15) | copy-start | bytes 772
  35.8 62.2 %copy-start = (s32[64,2]{0,1:T(2,128)S(1)}, s32[64,2]{0,1:T(2,128)}, u32[]{:S(2)}) copy-start(s32[64,2]{0,1:T(2,128)} %param.14) | copy-start | bytes 1540
